TPU v7x, 32 devices: a whole 2x2x4 slice. The times are simulated.
32 devices in a mesh: tf: 4 (over y, x), gz: 4 (over z), sec: 2 (over core).
Axes of the slice: x: 2, y: 2, z: 4, core: 2. Of those that a mesh axis runs over, the one named last changes fastest.
Arguments:
- residuals: bfloat16 [3, 4, 4, 2, 4, 8192], P(None, 'tf', 'gz', 'sec'), may hold values from -6 to 6
- weights: bfloat16 [4, 4, 2, 4, 8192], P('tf', 'gz', 'sec'), may hold values from 0.5 to 2
- fraction: bfloat16 [4, 4, 2, 4, 8192], P('tf', 'gz', 'sec'), may hold values from 0 to 1
- voxels: int32 [3, 4, 4, 2, 4, 8192], P(None, 'tf', 'gz', 'sec'), may hold values from 0 to 255, as said below
- kernel_reach: int32 [152], P('sec'), may hold values from 1 to 4
Outputs:
- distortion: float32 [3, 256, 152, 180], P(None, ('tf', 'gz'), 'sec')
Inputs may be any that keep to these rules, and one draw needn't show every extreme that they name: `voxels`: component 0 is the pad row, 1 the pad bin, 2 the drift bin. A residual at sec index s has its row in s * 76 to s * 76 + 75; its pad bin is at most 178; a residual at gz index g in slot t of the fifth dimension has its drift bin in block t * (number of gz devices) + g, that is among the 16 bins from (t * (number of gz devices) + g) * 16 on.
All inputs are finite; a program needn't handle non-finite values.
Results may differ from a plain program's by a relative error of at most 0.0026.
Values may be sent and summed in bfloat16 or wider, within the bound.
A program may use at most 64 MiB of HBM per device.

v0:
```python
import jax
import jax.numpy as jnp
from jax import lax
from jax.sharding import PartitionSpec as P

PAD = 180
DRIFT = 256


def entering(x, axis, combine, identity):
    devices, here = (lax.axis_size(axis), lax.axis_index(axis))
    everything = lax.all_gather(x, axis)
    start = jnp.broadcast_to(jnp.asarray(identity, x.dtype), x.shape)

    def hop(k, before):
        reached = k < here
        new = combine(before, everything[k])
        return jnp.where(reached, new, before)

    return lax.fori_loop(0, devices, hop, start)


def with_halo(block, sides, width):
    for axis, dim in sides:
        count = lax.axis_size(axis)
        forward = [(i, i + 1) for i in range(count - 1)]
        backward = [(target, source) for source, target in forward]
        low = lax.ppermute(
            lax.slice_in_dim(block, block.shape[dim] - width, None, axis=dim), axis, forward
        )
        high = lax.ppermute(lax.slice_in_dim(block, 0, width, axis=dim), axis, backward)
        block = jnp.concatenate([low, block, high], axis=dim)
    return block


def row_kernels(kernel_reach):
    spread = kernel_reach.astype(jnp.float32)[:, None, None]
    places = lax.broadcasted_iota(jnp.int32, (PAD, PAD), 0)
    others = lax.broadcasted_iota(jnp.int32, (PAD, PAD), 1)
    distance = jnp.abs(places - others).astype(jnp.float32)[None]
    return jnp.maximum(spread + 1.0 - distance, 0.0) / ((spread + 1.0) * (spread + 1.0))


def fill_slots(packed, floats, cell_count):
    blocks = packed.shape[0]
    slot_count = packed.shape[1]
    block_len = min(512, slot_count)
    pad_iota = lax.broadcasted_iota(jnp.int32, (1, 1, 1, PAD), 3)
    cell_iota = lax.broadcasted_iota(jnp.int32, (1, 1, cell_count), 2)
    nothing = jnp.zeros((), jnp.bfloat16)

    def advance(number, summed):
        index_part = lax.dynamic_slice_in_dim(packed, number * block_len, block_len, 1)
        value_part = lax.dynamic_slice_in_dim(floats, number * block_len, block_len, 2).astype(
            jnp.float32
        )
        cell_ids = index_part // PAD
        pad_ids = index_part - cell_ids * PAD
        weight_now = value_part[:, 3]
        left_share = weight_now * (1.0 - value_part[:, 4])
        right_share = weight_now * value_part[:, 4]
        left_chan = jnp.stack(
            [
                left_share,
                left_share * value_part[:, 0],
                left_share * value_part[:, 1],
                left_share * value_part[:, 2],
            ],
            2,
        ).astype(jnp.bfloat16)
        right_chan = jnp.stack(
            [
                right_share,
                right_share * value_part[:, 0],
                right_share * value_part[:, 1],
                right_share * value_part[:, 2],
            ],
            2,
        ).astype(jnp.bfloat16)
        at_left = pad_iota == pad_ids[:, :, None, None]
        at_right = pad_iota == pad_ids[:, :, None, None] + 1
        deposit = jnp.where(at_left, left_chan[..., None], nothing) + jnp.where(
            at_right, right_chan[..., None], nothing
        )
        deposit = deposit.reshape(blocks, block_len, 4 * PAD)
        onehot = (cell_iota == cell_ids[:, :, None]).astype(jnp.bfloat16)
        return summed + jnp.einsum(
            "tnk,tnc->tkc", onehot, deposit, preferred_element_type=jnp.float32
        )

    initial = jnp.zeros((blocks, cell_count, 4 * PAD), jnp.float32)
    return lax.fori_loop(0, slot_count // block_len, advance, initial)


def add_terms(earlier, later):
    return earlier + later


def accumulate(field):
    totals = jnp.sum(field, axis=1)
    carried = entering(totals, ("tf", "gz"), add_terms, jnp.zeros_like(totals))
    return carried[:, None] + jnp.cumsum(field, axis=1)


def smooth(field, kernel_reach):
    across = jnp.einsum(
        "kzrq,rpq->kzrp", field, row_kernels(kernel_reach), precision=lax.Precision.HIGHEST
    )
    rimmed = with_halo(across, (("sec", 2),), 2)
    row_total = across.shape[2]
    return (
        rimmed[:, :, 0:row_total]
        + 2.0 * rimmed[:, :, 1 : row_total + 1]
        + 3.0 * rimmed[:, :, 2 : row_total + 2]
        + 2.0 * rimmed[:, :, 3 : row_total + 3]
        + rimmed[:, :, 4 : row_total + 4]
    ) / 9.0


def per_device(residuals, weights, fraction, voxels, kernel_reach):
    gz_count = lax.axis_size("gz")
    drift_dev = DRIFT // (lax.axis_size("tf") * gz_count)
    row_dev = kernel_reach.shape[0]
    cell_count = drift_dev * row_dev
    coords = voxels[:, 0, 0, 0]
    target = lax.broadcasted_iota(jnp.int32, coords.shape[1:], 0)
    local_row = coords[0] - lax.axis_index("sec") * row_dev
    local_drift = coords[2] - (target * gz_count + lax.axis_index("gz")) * drift_dev
    packed = (local_drift * row_dev + local_row) * PAD + coords[1]
    floats = jnp.concatenate(
        [residuals[:, 0, 0, 0], weights[0, 0, 0][None], fraction[0, 0, 0][None]], 0
    )
    floats = jnp.transpose(floats, (1, 0, 2))
    block_count = drift_dev * lax.axis_size("tf") // drift_dev
    partial_sum = fill_slots(packed, floats, cell_count)
    histogram = lax.psum_scatter(
        partial_sum.reshape(block_count * drift_dev, row_dev, 4 * PAD),
        "tf",
        scatter_dimension=0,
        tiled=True,
    )
    histogram = histogram.reshape(drift_dev, row_dev, 4, PAD)
    means = histogram[:, :, 1:4] / (histogram[:, :, 0:1] + 1.0)
    means = jnp.transpose(means, (2, 0, 1, 3))
    result = accumulate(smooth(means, kernel_reach))
    return result


def solution(mesh):
    placed = (
        P(None, "tf", "gz", "sec", None, None),
        P("tf", "gz", "sec", None, None),
        P("tf", "gz", "sec", None, None),
        P(None, "tf", "gz", "sec", None, None),
        P("sec"),
    )
    return jax.shard_map(
        per_device,
        mesh=mesh,
        in_specs=placed,
        out_specs=P(None, ("tf", "gz"), "sec", None),
        check_vma=False,
    )
```

profile of v0, /device:TPU:0, one launch (start us, length us, event | category | flops | bytes accessed | tf_op | source)
XLA Modules:
  0.0 596.7 jit_solution(14019303874763572496)
XLA Ops:
  11.1 253.5 %while.32 = (s32[]{:T(128)}, f32[4,1216,720]{1,2,0:T(8,128)}, s32[4,8192]{1,0:T(4,128)S(1)}, bf16[4,5,8192]{2,1,0:T(8,128)(2,1)S(1)}, s32[]{:T(128)}, /*index=5*/s32[]{:T(128)}, s32[]{:T(128)}, s32[]{:T(128)}) while((s32[]{:T(128)}, f32[4,1216,720]{1,2,0:T(8,128)}, s32[4,8192]{1,0:T(4,128)S(1)}, ...), condition=%wide.region_1.2_spmd.clone.clone, body=%wide.region_0.1_spmd.clone.clone.sunk | while | flops 3600984064 | bytes 42660044 | solution.py:92
  12.7 2.3 add.232
  14.9 10.1 %select_add_fusion.5 = f32[4,1216,720]{1,2,0:T(8,128)} fusion(f32[4,1216,720]{1,2,0:T(8,128)} %get-tuple-element.431, bf16[4,512,720]{1,2,0:T(8,128)(2,1)} %add.232, pred[]{:T(512)S(6)} %compare.7, s32[4,512]{1,0:T(4,128)S(1)} %get-tuple-element.421), kind=kOutput, calls=%fused_computation.3.clone.1 | convolution fusion | flops 3595624448 | bytes 30973952 | tf_op jit(solution)/shard_map/while/body/eval_jaxpr/tnk,tnc->tkc/dot_general | solution.py:87
  26.6 2.3 add.232
  28.8 12.2 %select_add_fusion.5 = f32[4,1216,720]{1,2,0:T(8,128)} fusion(f32[4,1216,720]{1,2,0:T(8,128)} %get-tuple-element.431, bf16[4,512,720]{1,2,0:T(8,128)(2,1)} %add.232, pred[]{:T(512)S(6)} %compare.7, s32[4,512]{1,0:T(4,128)S(1)} %get-tuple-element.421), kind=kOutput, calls=%fused_computation.3.clone.1 | convolution fusion | flops 3595624448 | bytes 30973952 | tf_op jit(solution)/shard_map/while/body/eval_jaxpr/tnk,tnc->tkc/dot_general | solution.py:87
  42.5 2.3 add.232
  44.8 12.2 %select_add_fusion.5 = f32[4,1216,720]{1,2,0:T(8,128)} fusion(f32[4,1216,720]{1,2,0:T(8,128)} %get-tuple-element.431, bf16[4,512,720]{1,2,0:T(8,128)(2,1)} %add.232, pred[]{:T(512)S(6)} %compare.7, s32[4,512]{1,0:T(4,128)S(1)} %get-tuple-element.421), kind=kOutput, calls=%fused_computation.3.clone.1 | convolution fusion | flops 3595624448 | bytes 30973952 | tf_op jit(solution)/shard_map/while/body/eval_jaxpr/tnk,tnc->tkc/dot_general | solution.py:87
  60.8 12.2 %select_add_fusion.5 = f32[4,1216,720]{1,2,0:T(8,128)} fusion(f32[4,1216,720]{1,2,0:T(8,128)} %get-tuple-element.431, bf16[4,512,720]{1,2,0:T(8,128)(2,1)} %add.232, pred[]{:T(512)S(6)} %compare.7, s32[4,512]{1,0:T(4,128)S(1)} %get-tuple-element.421), kind=kOutput, calls=%fused_computation.3.clone.1 | convolution fusion | flops 3595624448 | bytes 30973952 | tf_op jit(solution)/shard_map/while/body/eval_jaxpr/tnk,tnc->tkc/dot_general | solution.py:87
  76.7 12.2 %select_add_fusion.5 = f32[4,1216,720]{1,2,0:T(8,128)} fusion(f32[4,1216,720]{1,2,0:T(8,128)} %get-tuple-element.431, bf16[4,512,720]{1,2,0:T(8,128)(2,1)} %add.232, pred[]{:T(512)S(6)} %compare.7, s32[4,512]{1,0:T(4,128)S(1)} %get-tuple-element.421), kind=kOutput, calls=%fused_computation.3.clone.1 | convolution fusion | flops 3595624448 | bytes 30973952 | tf_op jit(solution)/shard_map/while/body/eval_jaxpr/tnk,tnc->tkc/dot_general | solution.py:87
  92.7 12.2 %select_add_fusion.5 = f32[4,1216,720]{1,2,0:T(8,128)} fusion(f32[4,1216,720]{1,2,0:T(8,128)} %get-tuple-element.431, bf16[4,512,720]{1,2,0:T(8,128)(2,1)} %add.232, pred[]{:T(512)S(6)} %compare.7, s32[4,512]{1,0:T(4,128)S(1)} %get-tuple-element.421), kind=kOutput, calls=%fused_computation.3.clone.1 | convolution fusion | flops 3595624448 | bytes 30973952 | tf_op jit(solution)/shard_map/while/body/eval_jaxpr/tnk,tnc->tkc/dot_general | solution.py:87
  108.7 12.2 %select_add_fusion.5 = f32[4,1216,720]{1,2,0:T(8,128)} fusion(f32[4,1216,720]{1,2,0:T(8,128)} %get-tuple-element.431, bf16[4,512,720]{1,2,0:T(8,128)(2,1)} %add.232, pred[]{:T(512)S(6)} %compare.7, s32[4,512]{1,0:T(4,128)S(1)} %get-tuple-element.421), kind=kOutput, calls=%fused_computation.3.clone.1 | convolution fusion | flops 3595624448 | bytes 30973952 | tf_op jit(solution)/shard_map/while/body/eval_jaxpr/tnk,tnc->tkc/dot_general | solution.py:87
  124.7 12.2 %select_add_fusion.5 = f32[4,1216,720]{1,2,0:T(8,128)} fusion(f32[4,1216,720]{1,2,0:T(8,128)} %get-tuple-element.431, bf16[4,512,720]{1,2,0:T(8,128)(2,1)} %add.232, pred[]{:T(512)S(6)} %compare.7, s32[4,512]{1,0:T(4,128)S(1)} %get-tuple-element.421), kind=kOutput, calls=%fused_computation.3.clone.1 | convolution fusion | flops 3595624448 | bytes 30973952 | tf_op jit(solution)/shard_map/while/body/eval_jaxpr/tnk,tnc->tkc/dot_general | solution.py:87
  140.6 12.2 %select_add_fusion.5 = f32[4,1216,720]{1,2,0:T(8,128)} fusion(f32[4,1216,720]{1,2,0:T(8,128)} %get-tuple-element.431, bf16[4,512,720]{1,2,0:T(8,128)(2,1)} %add.232, pred[]{:T(512)S(6)} %compare.7, s32[4,512]{1,0:T(4,128)S(1)} %get-tuple-element.421), kind=kOutput, calls=%fused_computation.3.clone.1 | convolution fusion | flops 3595624448 | bytes 30973952 | tf_op jit(solution)/shard_map/while/body/eval_jaxpr/tnk,tnc->tkc/dot_general | solution.py:87
  156.6 12.2 %select_add_fusion.5 = f32[4,1216,720]{1,2,0:T(8,128)} fusion(f32[4,1216,720]{1,2,0:T(8,128)} %get-tuple-element.431, bf16[4,512,720]{1,2,0:T(8,128)(2,1)} %add.232, pred[]{:T(512)S(6)} %compare.7, s32[4,512]{1,0:T(4,128)S(1)} %get-tuple-element.421), kind=kOutput, calls=%fused_computation.3.clone.1 | convolution fusion | flops 3595624448 | bytes 30973952 | tf_op jit(solution)/shard_map/while/body/eval_jaxpr/tnk,tnc->tkc/dot_general | solution.py:87
  172.6 12.2 %select_add_fusion.5 = f32[4,1216,720]{1,2,0:T(8,128)} fusion(f32[4,1216,720]{1,2,0:T(8,128)} %get-tuple-element.431, bf16[4,512,720]{1,2,0:T(8,128)(2,1)} %add.232, pred[]{:T(512)S(6)} %compare.7, s32[4,512]{1,0:T(4,128)S(1)} %get-tuple-element.421), kind=kOutput, calls=%fused_computation.3.clone.1 | convolution fusion | flops 3595624448 | bytes 30973952 | tf_op jit(solution)/shard_map/while/body/eval_jaxpr/tnk,tnc->tkc/dot_general | solution.py:87
  188.6 12.2 %select_add_fusion.5 = f32[4,1216,720]{1,2,0:T(8,128)} fusion(f32[4,1216,720]{1,2,0:T(8,128)} %get-tuple-element.431, bf16[4,512,720]{1,2,0:T(8,128)(2,1)} %add.232, pred[]{:T(512)S(6)} %compare.7, s32[4,512]{1,0:T(4,128)S(1)} %get-tuple-element.421), kind=kOutput, calls=%fused_computation.3.clone.1 | convolution fusion | flops 3595624448 | bytes 30973952 | tf_op jit(solution)/shard_map/while/body/eval_jaxpr/tnk,tnc->tkc/dot_general | solution.py:87
  204.5 12.2 %select_add_fusion.5 = f32[4,1216,720]{1,2,0:T(8,128)} fusion(f32[4,1216,720]{1,2,0:T(8,128)} %get-tuple-element.431, bf16[4,512,720]{1,2,0:T(8,128)(2,1)} %add.232, pred[]{:T(512)S(6)} %compare.7, s32[4,512]{1,0:T(4,128)S(1)} %get-tuple-element.421), kind=kOutput, calls=%fused_computation.3.clone.1 | convolution fusion | flops 3595624448 | bytes 30973952 | tf_op jit(solution)/shard_map/while/body/eval_jaxpr/tnk,tnc->tkc/dot_general | solution.py:87
  220.5 12.2 %select_add_fusion.5 = f32[4,1216,720]{1,2,0:T(8,128)} fusion(f32[4,1216,720]{1,2,0:T(8,128)} %get-tuple-element.431, bf16[4,512,720]{1,2,0:T(8,128)(2,1)} %add.232, pred[]{:T(512)S(6)} %compare.7, s32[4,512]{1,0:T(4,128)S(1)} %get-tuple-element.421), kind=kOutput, calls=%fused_computation.3.clone.1 | convolution fusion | flops 3595624448 | bytes 30973952 | tf_op jit(solution)/shard_map/while/body/eval_jaxpr/tnk,tnc->tkc/dot_general | solution.py:87
  236.5 12.2 %select_add_fusion.5 = f32[4,1216,720]{1,2,0:T(8,128)} fusion(f32[4,1216,720]{1,2,0:T(8,128)} %get-tuple-element.431, bf16[4,512,720]{1,2,0:T(8,128)(2,1)} %add.232, pred[]{:T(512)S(6)} %compare.7, s32[4,512]{1,0:T(4,128)S(1)} %get-tuple-element.421), kind=kOutput, calls=%fused_computation.3.clone.1 | convolution fusion | flops 3595624448 | bytes 30973952 | tf_op jit(solution)/shard_map/while/body/eval_jaxpr/tnk,tnc->tkc/dot_general | solution.py:87
  252.5 12.2 %select_add_fusion.5 = f32[4,1216,720]{1,2,0:T(8,128)} fusion(f32[4,1216,720]{1,2,0:T(8,128)} %get-tuple-element.431, bf16[4,512,720]{1,2,0:T(8,128)(2,1)} %add.232, pred[]{:T(512)S(6)} %compare.7, s32[4,512]{1,0:T(4,128)S(1)} %get-tuple-element.421), kind=kOutput, calls=%fused_computation.3.clone.1 | convolution fusion | flops 3595624448 | bytes 30973952 | tf_op jit(solution)/shard_map/while/body/eval_jaxpr/tnk,tnc->tkc/dot_general | solution.py:87
  264.7 15.1 %copy.20 = f32[4,1216,720]{2,1,0:T(8,128)} copy(f32[4,1216,720]{1,2,0:T(8,128)} %get-tuple-element.242) | data formatting | bytes 28016640 | tf_op jit(solution)/shard_map/while | solution.py:92
  279.8 14.9 %reshape.444 = f32[64,76,720]{2,1,0:T(8,128)} reshape(f32[4,1216,720]{2,1,0:T(8,128)} %copy.20) | data formatting | bytes 28016640 | tf_op jit(solution)/shard_map/reshape | solution.py:137
  295.4 148.8 %reduce-scatter.2.cloned.1.call-done = f32[16,76,720]{2,1,0:T(8,128)} async-done(((f32[64,76,720]{2,1,0:T(8,128)}), f32[16,76,720]{2,1,0:T(8,128)}) %reduce-scatter.2.cloned.1.call-update) | async-done | bytes 3502096 | tf_op jit(solution)/shard_map/reduce_scatter | solution.py:136
  444.1 6.1 %copy.21 = f32[16,76,720]{2,0,1:T(8,128)} copy(f32[16,76,720]{2,1,0:T(8,128)} %reduce-scatter.2.cloned.1.call-done) | data formatting | bytes 7004160 | tf_op jit(solution)/shard_map/reduce_scatter | solution.py:136
  450.3 7.1 %reshape.445 = f32[16,76,4,180]{3,2,0,1:T(4,128)} reshape(f32[16,76,720]{2,0,1:T(8,128)} %copy.21) | data formatting | bytes 7004160 | tf_op jit(solution)/shard_map/reshape | solution.py:142
  457.4 3.9 slice_add_fusion
  464.4 16.2 %fusion.8 = f32[76,180,48]{1,2,0:S(1)} fusion(f32[76,180,48]{1,2,0:T(8,128)S(1)} %bitcast.84, f32[76]{0:T(128)S(1)} %get-tuple-element.337, f32[180,180]{1,0:T(8,128)S(1)} %abs_convert_fusion, f32[76]{0:T(128)S(1)} %get-tuple-element.336), kind=kOutput, calls=%fused_computation.33 | convolution fusion | flops 1425729536 | bytes 5383328
  485.6 4.3 fusion.34
  490.7 74.1 %all-gather.3.cloned.1.call-done = f32[48,76,180]{2,1,0:T(8,128)} async-done(((f32[3,76,180]{2,1,0:T(8,128)}), f32[48,76,180]{2,1,0:T(8,128)}) %all-gather.3.cloned.1.call-update) | async-done | bytes 2626576 | tf_op jit(solution)/shard_map/all_gather | solution.py:12
  564.8 16.9 %while.31 = (s32[]{:T(128)}, f32[3,76,180]{2,1,0:T(8,128)S(1)}, s32[]{:T(128)}, f32[16,3,76,180]{3,2,1,0:T(8,128)}, s32[]{:T(128)}, /*index=5*/s32[]{:T(128)}) while((s32[]{:T(128)}, f32[3,76,180]{2,1,0:T(8,128)S(1)}, s32[]{:T(128)}, f32[16,3,76,180]{3,2,1,0:T(8,128)}, s32[]{:T(128)}, /*index=5*/s32[]{:T(128)}) %tuple.108), condition=%wide.region_5.6_spmd.clone, body=%wide.region_4.5_spmd.clone.sunk | while | flops 123124 | bytes 492573 | solution.py:20
  581.6 4.2 broadcast_add_fusion.1
  585.9 4.0 copy.25
  (232 shorter events, 83.4 us)
Async XLA Ops:
  6.5 437.6 %reduce-scatter.2.cloned.1.call-start = ((), (), s32[]{:S(2)}) async-start(), calls=%async_computation.1 | async-start | bytes 19660800 | tf_op jit(solution)/shard_map/reduce_scatter | solution.py:136
  11.1 0.7 copy-start.1
  14.9 10.1 %copy-start.2 = (s32[4,8192]{1,0:T(4,128)S(1)}, s32[4,8192]{1,0:T(4,128)}, u32[]{:S(2)}) copy-start(s32[4,8192]{1,0:T(4,128)} %copy-done.1) | copy-start | bytes 393220 | tf_op jit(solution)/shard_map/while
  25.0 0.7 copy-start.1
  28.8 12.2 %copy-start.2 = (s32[4,8192]{1,0:T(4,128)S(1)}, s32[4,8192]{1,0:T(4,128)}, u32[]{:S(2)}) copy-start(s32[4,8192]{1,0:T(4,128)} %copy-done.1) | copy-start | bytes 393220 | tf_op jit(solution)/shard_map/while
  41.0 0.7 copy-start.1
  44.8 12.2 %copy-start.2 = (s32[4,8192]{1,0:T(4,128)S(1)}, s32[4,8192]{1,0:T(4,128)}, u32[]{:S(2)}) copy-start(s32[4,8192]{1,0:T(4,128)} %copy-done.1) | copy-start | bytes 393220 | tf_op jit(solution)/shard_map/while
  57.0 0.7 copy-start.1
  60.8 12.2 %copy-start.2 = (s32[4,8192]{1,0:T(4,128)S(1)}, s32[4,8192]{1,0:T(4,128)}, u32[]{:S(2)}) copy-start(s32[4,8192]{1,0:T(4,128)} %copy-done.1) | copy-start | bytes 393220 | tf_op jit(solution)/shard_map/while
  73.0 0.7 copy-start.1
  76.7 12.2 %copy-start.2 = (s32[4,8192]{1,0:T(4,128)S(1)}, s32[4,8192]{1,0:T(4,128)}, u32[]{:S(2)}) copy-start(s32[4,8192]{1,0:T(4,128)} %copy-done.1) | copy-start | bytes 393220 | tf_op jit(solution)/shard_map/while
  88.9 0.7 copy-start.1
  92.7 12.2 %copy-start.2 = (s32[4,8192]{1,0:T(4,128)S(1)}, s32[4,8192]{1,0:T(4,128)}, u32[]{:S(2)}) copy-start(s32[4,8192]{1,0:T(4,128)} %copy-done.1) | copy-start | bytes 393220 | tf_op jit(solution)/shard_map/while
  104.9 0.7 copy-start.1
  108.7 12.2 %copy-start.2 = (s32[4,8192]{1,0:T(4,128)S(1)}, s32[4,8192]{1,0:T(4,128)}, u32[]{:S(2)}) copy-start(s32[4,8192]{1,0:T(4,128)} %copy-done.1) | copy-start | bytes 393220 | tf_op jit(solution)/shard_map/while
  120.9 0.7 copy-start.1
  124.7 12.2 %copy-start.2 = (s32[4,8192]{1,0:T(4,128)S(1)}, s32[4,8192]{1,0:T(4,128)}, u32[]{:S(2)}) copy-start(s32[4,8192]{1,0:T(4,128)} %copy-done.1) | copy-start | bytes 393220 | tf_op jit(solution)/shard_map/while
  136.9 0.7 copy-start.1
  140.6 12.2 %copy-start.2 = (s32[4,8192]{1,0:T(4,128)S(1)}, s32[4,8192]{1,0:T(4,128)}, u32[]{:S(2)}) copy-start(s32[4,8192]{1,0:T(4,128)} %copy-done.1) | copy-start | bytes 393220 | tf_op jit(solution)/shard_map/while
  152.8 0.7 copy-start.1
  156.6 12.2 %copy-start.2 = (s32[4,8192]{1,0:T(4,128)S(1)}, s32[4,8192]{1,0:T(4,128)}, u32[]{:S(2)}) copy-start(s32[4,8192]{1,0:T(4,128)} %copy-done.1) | copy-start | bytes 393220 | tf_op jit(solution)/shard_map/while
  172.6 12.2 %copy-start.2 = (s32[4,8192]{1,0:T(4,128)S(1)}, s32[4,8192]{1,0:T(4,128)}, u32[]{:S(2)}) copy-start(s32[4,8192]{1,0:T(4,128)} %copy-done.1) | copy-start | bytes 393220 | tf_op jit(solution)/shard_map/while
  188.6 12.2 %copy-start.2 = (s32[4,8192]{1,0:T(4,128)S(1)}, s32[4,8192]{1,0:T(4,128)}, u32[]{:S(2)}) copy-start(s32[4,8192]{1,0:T(4,128)} %copy-done.1) | copy-start | bytes 393220 | tf_op jit(solution)/shard_map/while
  204.5 12.2 %copy-start.2 = (s32[4,8192]{1,0:T(4,128)S(1)}, s32[4,8192]{1,0:T(4,128)}, u32[]{:S(2)}) copy-start(s32[4,8192]{1,0:T(4,128)} %copy-done.1) | copy-start | bytes 393220 | tf_op jit(solution)/shard_map/while
  220.5 12.2 %copy-start.2 = (s32[4,8192]{1,0:T(4,128)S(1)}, s32[4,8192]{1,0:T(4,128)}, u32[]{:S(2)}) copy-start(s32[4,8192]{1,0:T(4,128)} %copy-done.1) | copy-start | bytes 393220 | tf_op jit(solution)/shard_map/while
  236.5 12.2 %copy-start.2 = (s32[4,8192]{1,0:T(4,128)S(1)}, s32[4,8192]{1,0:T(4,128)}, u32[]{:S(2)}) copy-start(s32[4,8192]{1,0:T(4,128)} %copy-done.1) | copy-start | bytes 393220 | tf_op jit(solution)/shard_map/while
  252.5 12.2 %copy-start.2 = (s32[4,8192]{1,0:T(4,128)S(1)}, s32[4,8192]{1,0:T(4,128)}, u32[]{:S(2)}) copy-start(s32[4,8192]{1,0:T(4,128)} %copy-done.1) | copy-start | bytes 393220 | tf_op jit(solution)/shard_map/while
  294.7 0.7 copy-start.3
  294.8 270.0 %all-gather.3.cloned.1.call-start = ((), (), s32[]{:S(2)}) async-start(), calls=%async_computation.2 | async-start | bytes 4177920 | tf_op jit(solution)/shard_map/all_gather | solution.py:12
  457.4 4.0 copy-start
  480.7 3.1 collective-permute-start
  482.4 3.2 collective-permute-start.1
  (6 other events, 3.9 us)
Sparse Core Ops, SparseCore 0:
  294.9 149.2 reduce-scatter.1
  490.8 73.9 all-gather.2
where the time goes:
time: 598 us; the launch traced here: 597 us
  waiting for transfers between devices  225 us (38%)
  matrix products  209 us (35%)
  local copies, waits for them, and re-layouts  89.1 us (15%)
  other arithmetic  55.9 us (9%)
  between operations  13.5 us (2%)
    dot_general x16, matrix products, advance(): jnp.einsum('tnk,tnc->tkc', onehot, deposit, preferred_element_type=jnp.fl...  193 us
    reduce_scatter x1, waiting for transfers between devices, per_device(): lax.psum_scatter(partial_sum.reshape(block_count * drift_dev, row_dev, 4...  149 us
    all_gather x1, waiting for transfers between devices, entering(): everything = lax.all_gather(x, axis)  74.1 us
    add x16, local copies, waits for them, and re-layouts, advance(): jnp.where(at_left, left_chan[..., None], nothing)  36.2 us
    select_n x16, other arithmetic, hop(): return jnp.where(reached, new, before)  16.5 us
    unnamed x1, matrix products  16.2 us
    while x1, local copies, waits for them, and re-layouts, fill_slots(): return lax.fori_loop(0, slot_count // block_len, advance, initial)  15.1 us
    reshape x1, local copies, waits for them, and re-layouts, per_device(): partial_sum.reshape(block_count * drift_dev, row_dev, 4 * PAD)  14.9 us
  transfers between devices with their start and end apart: 4, of which 3 were waited for; matrix products, arithmetic and copies ran while one was open for 0% of the time, Pallas kernels for 0%

commit v1 on v0

v1 whole, which is shorter than its diff:
```python
import functools

import jax
import jax.numpy as jnp
from jax import lax
from jax.experimental import pallas as pl
from jax.experimental.pallas import tpu as pltpu
from jax.sharding import PartitionSpec as P

PAD = 180
DRIFT = 256
PADS = 192
LANES = 256
TAPS = 5
MESH = pl.DeviceIdType.MESH
F32 = jnp.float32
BF16 = jnp.bfloat16


def round_up(value, unit):
    return (value + unit - 1) // unit * unit


def kernel(
    sizes,
    res_ref,
    weight_ref,
    frac_ref,
    vox_ref,
    reach_ref,
    out_ref,
    send_buf,
    recv_buf,
    hist,
    field,
    taps,
    low_out,
    high_out,
    low_in,
    high_in,
    last_out,
    last_in,
    totals,
    by_gz,
    by_tf,
    back,
    carry,
    res_send,
    res_recv,
    halo_send,
    halo_recv,
    scan_send,
    scan_recv,
):
    tf_count, gz_count, sec_count, drift_dev, row_dev, rows_pad, part, half, step = sizes
    my_tf = lax.axis_index("tf")
    my_gz = lax.axis_index("gz")
    my_sec = lax.axis_index("sec")
    has_low = my_sec > 0
    has_high = my_sec < sec_count - 1
    last = drift_dev - 1

    barrier = pltpu.get_barrier_semaphore()
    for s in range(1, tf_count):
        pl.semaphore_signal(
            barrier, inc=1, device_id={"tf": lax.rem(my_tf + s, tf_count)}, device_id_type=MESH
        )
    for s in range(1, gz_count):
        pl.semaphore_signal(
            barrier, inc=1, device_id={"gz": lax.rem(my_gz + s, gz_count)}, device_id_type=MESH
        )

    @pl.when(has_low)
    def _():
        pl.semaphore_signal(barrier, inc=1, device_id={"sec": my_sec - 1}, device_id_type=MESH)

    @pl.when(has_high)
    def _():
        pl.semaphore_signal(barrier, inc=1, device_id={"sec": my_sec + 1}, device_id_type=MESH)

    first_row = my_sec * row_dev
    channels = [res_ref[0], res_ref[1], res_ref[2], weight_ref[...], frac_ref[...]]
    channels = [c.astype(F32) for c in channels]
    channels.append((vox_ref[0] - first_row).astype(F32))
    channels.append(vox_ref[1].astype(F32))
    block_of = lax.broadcasted_iota(jnp.int32, vox_ref.shape[1:], 0)
    channels.append((vox_ref[2] - (block_of * gz_count + my_gz) * drift_dev).astype(F32))
    for t in range(tf_count):
        rows = [c[t : t + 1, h * half : (h + 1) * half] for h in range(2) for c in channels]
        send_buf[t] = jnp.concatenate(rows, axis=0).astype(BF16)

    neighbours = has_low.astype(jnp.int32) + has_high.astype(jnp.int32)
    pl.semaphore_wait(barrier, tf_count + gz_count - 2 + neighbours)

    def residual_copy(s):
        target = lax.rem(my_tf + s, tf_count)
        return pltpu.make_async_remote_copy(
            src_ref=send_buf.at[target],
            dst_ref=recv_buf.at[s],
            send_sem=res_send.at[s],
            recv_sem=res_recv.at[s],
            device_id={"tf": target},
            device_id_type=MESH,
        )

    for s in range(1, tf_count):
        residual_copy(s).start()
    recv_buf[0] = send_buf[my_tf]
    hist[...] = jnp.zeros_like(hist)

    reach = reach_ref[...].astype(F32)
    spread = jnp.broadcast_to(reach, (rows_pad, LANES)) + 1.0
    for d in range(TAPS):
        taps[d] = jnp.maximum(spread - float(d), 0.0) / (spread * spread * 9.0)

    steps = half // step
    width = 2 * step

    def deposit(number, _):
        s = number // steps
        j = number % steps

        @pl.when(jnp.logical_and(j == 0, s > 0))
        def _():
            residual_copy(s).wait_recv()

        block = recv_buf[s, :, pl.ds(pl.multiple_of(j * step, step), step)].astype(F32)
        data = jnp.concatenate([block[0:8], block[8:16]], axis=1)
        left = data[3:4] * (1.0 - data[4:5])
        right = data[3:4] * data[4:5]
        row_id = data[5:6].astype(BF16)
        pad_id = data[6:7].astype(BF16)
        next_id = (data[6:7] + 1.0).astype(BF16)
        drift_id = data[7:8]
        pad_iota = lax.broadcasted_iota(jnp.int32, (PADS, width), 0).astype(BF16)
        row_iota = lax.broadcasted_iota(jnp.int32, (rows_pad, width), 0).astype(BF16)
        at_left = pad_iota == pad_id
        at_right = pad_iota == next_id
        nothing = jnp.zeros((PADS, width), BF16)
        parts = []
        for c in range(4):
            l_val = left if c == 0 else left * data[c - 1 : c]
            r_val = right if c == 0 else right * data[c - 1 : c]
            l_all = jnp.broadcast_to(l_val.astype(BF16), (PADS, width))
            r_all = jnp.broadcast_to(r_val.astype(BF16), (PADS, width))
            parts.append(jnp.where(at_left, l_all, jnp.where(at_right, r_all, nothing)))
        columns = jnp.concatenate(parts, axis=0)
        at_row = jnp.where(
            row_iota == row_id,
            jnp.ones((rows_pad, width), BF16),
            jnp.zeros((rows_pad, width), BF16),
        )
        cells = []
        for z in range(drift_dev):
            chosen = jnp.where(drift_id == float(z), 1.0, 0.0).astype(BF16)
            cells.append(at_row * chosen)
        cells = jnp.concatenate(cells, axis=0)
        hist[...] += lax.dot_general(
            cells, columns, (((1,), (1,)), ((), ())), preferred_element_type=F32
        )
        return 0

    lax.fori_loop(0, tf_count * steps, deposit, 0)

    lane = lax.broadcasted_iota(jnp.int32, (rows_pad, LANES), 1)
    inside = lane < PAD
    field[:, last] = jnp.zeros((3, rows_pad, LANES), F32)

    def channel(z, c):
        start = c * PADS // 128 * 128
        rows = pl.ds(pl.multiple_of(z * rows_pad, rows_pad), rows_pad)
        piece = hist[rows, start : start + LANES]
        if c * PADS != start:
            piece = pltpu.roll(piece, LANES - (c * PADS - start), 1)
        return piece

    def average(z, _):
        before = jnp.where(z == 0, last, z - 1)
        scale = 1.0 / (channel(z, 0) + 1.0)
        for k in range(3):
            mean = jnp.where(inside, channel(z, k + 1) * scale, 0.0)
            field[k, z] = field[k, before] + mean
        return 0

    lax.fori_loop(0, drift_dev, average, 0)

    def across(k, z):
        x = field[k, z]
        total = taps[0] * x
        for d in range(1, TAPS):
            total += taps[d] * (pltpu.roll(x, d, 1) + pltpu.roll(x, LANES - d, 1))
        field[k, z] = total

    def down(k, z):
        x = field[k, z]
        near = pltpu.roll(x, 1, 0) + pltpu.roll(x, rows_pad - 1, 0)
        far = pltpu.roll(x, 2, 0) + pltpu.roll(x, rows_pad - 2, 0)
        return 3.0 * x + 2.0 * near + far

    def to_low(src, dst, i):
        return pltpu.make_async_remote_copy(
            src_ref=src, dst_ref=dst, send_sem=halo_send.at[i], recv_sem=halo_recv.at[i],
            device_id={"sec": my_sec - 1}, device_id_type=MESH,
        )

    def to_high(src, dst, i):
        return pltpu.make_async_remote_copy(
            src_ref=src, dst_ref=dst, send_sem=halo_send.at[i], recv_sem=halo_recv.at[i],
            device_id={"sec": my_sec + 1}, device_id_type=MESH,
        )

    last_out[...] = jnp.zeros_like(last_out)
    for k in range(3):
        across(k, last)
        for j in range(2):
            last_out[0, pl.ds(k * 2 + j, 1)] = field[k, last, pl.ds(j, 1)]
            last_out[1, pl.ds(k * 2 + j, 1)] = field[k, last, pl.ds(row_dev - 2 + j, 1)]
    last_low = to_low(last_out.at[0], last_in.at[1], 0)
    last_high = to_high(last_out.at[1], last_in.at[0], 1)
    both_low = to_low(low_out, high_in, 2)
    both_high = to_high(high_out, low_in, 3)

    @pl.when(has_low)
    def _():
        last_low.start()

    @pl.when(has_high)
    def _():
        last_high.start()

    def widen(z, _):
        for k in range(3):
            across(k, z)
            for j in range(2):
                low_out[j, k, pl.ds(z, 1)] = field[k, z, pl.ds(j, 1)]
                high_out[j, k, pl.ds(z, 1)] = field[k, z, pl.ds(row_dev - 2 + j, 1)]
        return 0

    @pl.when(has_high)
    def _():
        last_low.wait_recv()
        for k in range(3):
            field[k, last, pl.ds(row_dev, 2)] = last_in[1, pl.ds(k * 2, 2)]

    @pl.when(has_low)
    def _():
        last_high.wait_recv()
        for k in range(3):
            field[k, last, pl.ds(rows_pad - 2, 2)] = last_in[0, pl.ds(k * 2, 2)]

    totals[...] = jnp.zeros_like(totals)
    for k in range(3):
        totals[pl.ds(k * rows_pad, rows_pad)] = down(k, last)

    def first_copy(s):
        target = lax.rem(my_gz + s, gz_count)
        return pltpu.make_async_remote_copy(
            src_ref=totals.at[pl.ds(pl.multiple_of(target * part, part), part)],
            dst_ref=by_gz.at[my_gz],
            send_sem=scan_send.at[0, s], recv_sem=scan_recv.at[0, s],
            device_id={"gz": target}, device_id_type=MESH,
        )

    def second_copy(s):
        target = lax.rem(my_tf + s, tf_count)
        return pltpu.make_async_remote_copy(
            src_ref=by_tf.at[my_tf], dst_ref=by_tf.at[my_tf],
            send_sem=scan_send.at[1, s], recv_sem=scan_recv.at[1, s],
            device_id={"tf": target}, device_id_type=MESH,
        )

    def third_copy(s):
        target = lax.rem(my_gz + s, gz_count)
        return pltpu.make_async_remote_copy(
            src_ref=back.at[target],
            dst_ref=carry.at[pl.ds(pl.multiple_of(my_gz * part, part), part)],
            send_sem=scan_send.at[2, s], recv_sem=scan_recv.at[2, s],
            device_id={"gz": target}, device_id_type=MESH,
        )

    for s in range(1, gz_count):
        first_copy(s).start()
    by_gz[my_gz] = totals[pl.ds(pl.multiple_of(my_gz * part, part), part)]

    lax.fori_loop(0, last, widen, 0)

    @pl.when(has_low)
    def _():
        both_low.start()

    @pl.when(has_high)
    def _():
        both_high.start()

    for s in range(1, gz_count):
        first_copy(s).wait_recv()
    column = by_gz[0]
    for g in range(1, gz_count):
        column += by_gz[g]
    by_tf[my_tf] = column
    for s in range(1, tf_count):
        second_copy(s).start()

    @pl.when(has_high)
    def _():
        both_low.wait_recv()

    @pl.when(has_low)
    def _():
        both_high.wait_recv()

    def fill(z, _):
        @pl.when(has_high)
        def _():
            for k in range(3):
                for j in range(2):
                    field[k, z, pl.ds(row_dev + j, 1)] = high_in[j, k, pl.ds(z, 1)]

        @pl.when(has_low)
        def _():
            for k in range(3):
                for j in range(2):
                    field[k, z, pl.ds(rows_pad - 2 + j, 1)] = low_in[j, k, pl.ds(z, 1)]

        return 0

    lax.fori_loop(0, last, fill, 0)

    for s in range(1, tf_count):
        second_copy(s).wait_recv()
    base = jnp.zeros((part, LANES), F32)
    for t in range(tf_count):
        base += jnp.where(t < my_tf, by_tf[t], 0.0)
    for g in range(gz_count):
        back[g] = base
        base = base + by_gz[g]
    for s in range(1, gz_count):
        third_copy(s).start()
    carry[pl.ds(pl.multiple_of(my_gz * part, part), part)] = back[my_gz]

    def narrow(z, _):
        for k in range(3):
            field[k, z] = down(k, z)
        return 0

    lax.fori_loop(0, last, narrow, 0)
    for k in range(3):
        field[k, last] = totals[pl.ds(k * rows_pad, rows_pad)]

    for s in range(1, gz_count):
        third_copy(s).wait_recv()

    def finish(z, _):
        for k in range(3):
            whole = field[k, z] + carry[pl.ds(k * rows_pad, rows_pad)]
            out_ref[k, z] = whole[:row_dev, :PAD]
        return 0

    lax.fori_loop(0, drift_dev, finish, 0)

    for s in range(1, tf_count):
        residual_copy(s).wait_send()
        second_copy(s).wait_send()
    for s in range(1, gz_count):
        first_copy(s).wait_send()
        third_copy(s).wait_send()

    @pl.when(has_low)
    def _():
        last_low.wait_send()
        both_low.wait_send()

    @pl.when(has_high)
    def _():
        last_high.wait_send()
        both_high.wait_send()


def per_device(residuals, weights, fraction, voxels, kernel_reach):
    tf_count = lax.axis_size("tf")
    gz_count = lax.axis_size("gz")
    sec_count = lax.axis_size("sec")
    drift_dev = DRIFT // (tf_count * gz_count)
    row_dev = kernel_reach.shape[0]
    rows_pad = round_up(row_dev + 4, 16)
    part = round_up(-(-3 * rows_pad // gz_count), 8)
    slots = weights.shape[-1]
    half = slots // 2
    step = min(512, half)
    sizes = (tf_count, gz_count, sec_count, drift_dev, row_dev, rows_pad, part, half, step)
    reach = jnp.pad(kernel_reach, (0, rows_pad - row_dev), constant_values=1)[:, None]
    vmem = pl.BlockSpec(memory_space=pltpu.VMEM)
    bins = round_up(drift_dev, 8)
    return pl.pallas_call(
        functools.partial(kernel, sizes),
        out_shape=jax.ShapeDtypeStruct((3, drift_dev, row_dev, PAD), F32),
        in_specs=[vmem] * 5,
        out_specs=vmem,
        scratch_shapes=[
            pltpu.VMEM((tf_count, 16, half), BF16),
            pltpu.VMEM((tf_count, 16, half), BF16),
            pltpu.VMEM((drift_dev * rows_pad, 4 * PADS), F32),
            pltpu.VMEM((3, drift_dev, rows_pad, LANES), F32),
            pltpu.VMEM((TAPS, rows_pad, LANES), F32),
            pltpu.VMEM((2, 3, bins, LANES), F32),
            pltpu.VMEM((2, 3, bins, LANES), F32),
            pltpu.VMEM((2, 3, bins, LANES), F32),
            pltpu.VMEM((2, 3, bins, LANES), F32),
            pltpu.VMEM((2, 8, LANES), F32),
            pltpu.VMEM((2, 8, LANES), F32),
            pltpu.VMEM((gz_count * part, LANES), F32),
            pltpu.VMEM((gz_count, part, LANES), F32),
            pltpu.VMEM((tf_count, part, LANES), F32),
            pltpu.VMEM((gz_count, part, LANES), F32),
            pltpu.VMEM((gz_count * part, LANES), F32),
            pltpu.SemaphoreType.DMA((tf_count,)),
            pltpu.SemaphoreType.DMA((tf_count,)),
            pltpu.SemaphoreType.DMA((4,)),
            pltpu.SemaphoreType.DMA((4,)),
            pltpu.SemaphoreType.DMA((3, max(tf_count, gz_count))),
            pltpu.SemaphoreType.DMA((3, max(tf_count, gz_count))),
        ],
        compiler_params=pltpu.CompilerParams(
            collective_id=0, has_side_effects=True, vmem_limit_bytes=56 * 1024 * 1024
        ),
    )(
        residuals[:, 0, 0, 0],
        weights[0, 0, 0],
        fraction[0, 0, 0],
        voxels[:, 0, 0, 0],
        reach,
    )


def solution(mesh):
    placed = (
        P(None, "tf", "gz", "sec", None, None),
        P("tf", "gz", "sec", None, None),
        P("tf", "gz", "sec", None, None),
        P(None, "tf", "gz", "sec", None, None),
        P("sec"),
    )
    return jax.shard_map(
        per_device,
        mesh=mesh,
        in_specs=placed,
        out_specs=P(None, ("tf", "gz"), "sec", None),
        check_vma=False,
    )
```

time: 598 us -> 113 us (0.19)
  waiting for transfers between devices: 225 us -> 0 us
  matrix products: 209 us -> 0 us
  Pallas kernels: 0 us -> 105 us
  local copies, waits for them, and re-layouts: 89.1 us -> 7.51 us
  other arithmetic: 55.9 us -> 0 us
  between operations: 13.5 us -> 0.01 us
    dot_general x16 -> x0, matrix products: 193 us -> none  [advance(): jnp.einsum('tnk,tnc->tkc', onehot, deposit, preferred_element_type=jnp.fl...]
    reduce_scatter x1 -> x0, waiting for transfers between devices: 149 us -> none  [per_device(): lax.psum_scatter(partial_sum.reshape(block_count * drift_dev, row_dev, 4...]
    pallas_call x0 -> x1, Pallas kernels: none -> 105 us  [per_device(): pl.pallas_call(functools.partial(kernel, sizes), out_shape=jax.ShapeDtype...]
    all_gather x1 -> x0, waiting for transfers between devices: 74.1 us -> none  [entering(): everything = lax.all_gather(x, axis)]
    add x17 -> x0, local copies, waits for them, and re-layouts: 40.2 us -> none  [the longest x16 36.2 us: advance(): jnp.where(at_left, left_chan[..., None], nothing)]
    reshape x2 -> x0, local copies, waits for them, and re-layouts: 22 us -> none  [the longest x1 14.9 us: per_device(): partial_sum.reshape(block_count * drift_dev, row_dev, 4 * PAD)]
    add x35 -> x0, other arithmetic: 19.3 us -> none  [the longest x16 13.7 us: advance(): jnp.where(at_left, left_chan[..., None], nothing)]
    select_n x16 -> x0, other arithmetic: 16.5 us -> none  [hop(): return jnp.where(reached, new, before)]
  transfers between devices with their start and end apart: 4 -> 0, of which waited for: 3 -> 0; matrix products, arithmetic and copies ran while one was open for 0% -> 0% of each run, Pallas kernels for 0% -> 0%
where the time goes in v1:
time: 113 us
  Pallas kernels  105 us (93%)
  local copies, waits for them, and re-layouts  7.51 us (7%)
    pallas_call x1, Pallas kernels, per_device(): pl.pallas_call(functools.partial(kernel, sizes), out_shape=jax.ShapeDtype...  105 us
    pallas_call x1, local copies, waits for them, and re-layouts, per_device(): pl.pallas_call(functools.partial(kernel, sizes), out_shape=jax.ShapeDtype...  6.14 us

profile of v1, /device:TPU:0, one launch (start us, length us, event | category | flops | bytes accessed | tf_op | source)
XLA Modules:
  0.0 112.8 jit_solution(8160656949391625175)
XLA Ops:
  0.0 0.7 pad_bitcast_fusion
  0.7 0.7 copy.6.reach_ref
  1.4 105.2 %shard_map.55 = f32[3,16,76,180]{3,2,1,0:T(8,128)} custom-call(bf16[3,4,8192]{2,1,0:T(4,128)(2,1)} %bitcast.7, bf16[4,8192]{1,0:T(4,128)(2,1)} %bitcast.8, bf16[4,8192]{1,0:T(4,128)(2,1)} %bitcast.9, s32[3,4,8192]{2,1,0:T(4,128)} %bitcast.6, s32[80,1]{1,0:T(8,128)} %copy.6.reach_ref), custom_call_target="tpu_custom_call" | custom-call | tf_op jit(solution)/shard_map/pallas_call | solution.py:394
  106.6 6.1 %copy.7 = f32[3,16,76,180]{3,1,2,0:T(8,128)} copy(f32[3,16,76,180]{3,2,1,0:T(8,128)} %shard_map.55) | data formatting | bytes 5253120 | tf_op jit(solution)/shard_map/pallas_call | solution.py:394

commit v2 on v1

--- a/solution.py
+++ b/solution.py
@@ -31,13 +31,14 @@
     out_ref,
     send_buf,
     recv_buf,
+    cells_even,
+    cells_odd,
+    columns_even,
+    columns_odd,
     hist,
     field,
+    sums,
     taps,
-    low_out,
-    high_out,
-    low_in,
-    high_in,
     last_out,
     last_in,
     totals,
@@ -52,13 +53,16 @@
     scan_send,
     scan_recv,
 ):
-    tf_count, gz_count, sec_count, drift_dev, row_dev, rows_pad, part, half, step = sizes
+    tf_count, gz_count, sec_count, drift_dev, drift_pad, row_dev, rows_pad, part, half, step = sizes
     my_tf = lax.axis_index("tf")
     my_gz = lax.axis_index("gz")
     my_sec = lax.axis_index("sec")
     has_low = my_sec > 0
     has_high = my_sec < sec_count - 1
-    last = drift_dev - 1
+    group = 4 if row_dev % 4 == 0 else 1
+
+    for r in (0, 1, row_dev + 2, row_dev + 3):
+        field[:, r] = jnp.zeros((3, drift_pad, LANES), F32)
 
     barrier = pltpu.get_barrier_semaphore()
     for s in range(1, tf_count):
@@ -116,83 +120,97 @@
     steps = half // step
     width = 2 * step
 
-    def deposit(number, _):
+    total = tf_count * steps
+
+    def spread_out(number, cells, columns):
         s = number // steps
         j = number % steps
-
-        @pl.when(jnp.logical_and(j == 0, s > 0))
-        def _():
-            residual_copy(s).wait_recv()
-
         block = recv_buf[s, :, pl.ds(pl.multiple_of(j * step, step), step)].astype(F32)
         data = jnp.concatenate([block[0:8], block[8:16]], axis=1)
         left = data[3:4] * (1.0 - data[4:5])
         right = data[3:4] * data[4:5]
-        row_id = data[5:6].astype(BF16)
         pad_id = data[6:7].astype(BF16)
         next_id = (data[6:7] + 1.0).astype(BF16)
-        drift_id = data[7:8]
         pad_iota = lax.broadcasted_iota(jnp.int32, (PADS, width), 0).astype(BF16)
-        row_iota = lax.broadcasted_iota(jnp.int32, (rows_pad, width), 0).astype(BF16)
         at_left = pad_iota == pad_id
         at_right = pad_iota == next_id
         nothing = jnp.zeros((PADS, width), BF16)
-        parts = []
         for c in range(4):
             l_val = left if c == 0 else left * data[c - 1 : c]
             r_val = right if c == 0 else right * data[c - 1 : c]
             l_all = jnp.broadcast_to(l_val.astype(BF16), (PADS, width))
             r_all = jnp.broadcast_to(r_val.astype(BF16), (PADS, width))
-            parts.append(jnp.where(at_left, l_all, jnp.where(at_right, r_all, nothing)))
-        columns = jnp.concatenate(parts, axis=0)
-        at_row = jnp.where(
-            row_iota == row_id,
-            jnp.ones((rows_pad, width), BF16),
-            jnp.zeros((rows_pad, width), BF16),
-        )
-        cells = []
-        for z in range(drift_dev):
-            chosen = jnp.where(drift_id == float(z), 1.0, 0.0).astype(BF16)
-            cells.append(at_row * chosen)
-        cells = jnp.concatenate(cells, axis=0)
+            columns[c * PADS : (c + 1) * PADS] = jnp.where(
+                at_left, l_all, jnp.where(at_right, r_all, nothing)
+            )
+        tile = (drift_pad, width)
+        drift_iota = lax.broadcasted_iota(jnp.int32, tile, 0).astype(BF16)
+        at_drift = jnp.where(
+            drift_iota == data[7:8].astype(BF16), jnp.ones(tile, BF16), jnp.zeros(tile, BF16)
+        )
+        row_id = jnp.broadcast_to(data[5:6].astype(BF16), tile)
+        for r in range(row_dev):
+            cells[r * drift_pad : (r + 1) * drift_pad] = jnp.where(
+                row_id == jnp.full(tile, r, BF16), at_drift, jnp.zeros(tile, BF16)
+            )
+
+    def add_up(cells, columns):
         hist[...] += lax.dot_general(
-            cells, columns, (((1,), (1,)), ((), ())), preferred_element_type=F32
-        )
+            cells[...], columns[...], (((1,), (1,)), ((), ())), preferred_element_type=F32
+        )
+
+    spread_out(0, cells_even, columns_even)
+
+    def deposit(pair, _):
+        later = 2 * pair + 2
+
+        @pl.when(jnp.logical_and(later % steps == 0, later < total))
+        def _():
+            residual_copy(later // steps).wait_recv()
+
+        add_up(cells_even, columns_even)
+        spread_out(2 * pair + 1, cells_odd, columns_odd)
+        add_up(cells_odd, columns_odd)
+        spread_out(jnp.minimum(later, total - 1), cells_even, columns_even)
         return 0
 
-    lax.fori_loop(0, tf_count * steps, deposit, 0)
-
-    lane = lax.broadcasted_iota(jnp.int32, (rows_pad, LANES), 1)
-    inside = lane < PAD
-    field[:, last] = jnp.zeros((3, rows_pad, LANES), F32)
-
-    def channel(z, c):
+    lax.fori_loop(0, total // 2, deposit, 0)
+
+    inside = lax.broadcasted_iota(jnp.int32, (drift_pad, LANES), 1) < PAD
+    sums[...] = jnp.zeros_like(sums)
+
+    def channel(r, c):
         start = c * PADS // 128 * 128
-        rows = pl.ds(pl.multiple_of(z * rows_pad, rows_pad), rows_pad)
+        rows = pl.ds(pl.multiple_of(r * drift_pad, drift_pad), drift_pad)
         piece = hist[rows, start : start + LANES]
         if c * PADS != start:
             piece = pltpu.roll(piece, LANES - (c * PADS - start), 1)
         return piece
 
-    def average(z, _):
-        before = jnp.where(z == 0, last, z - 1)
-        scale = 1.0 / (channel(z, 0) + 1.0)
+    def each_row(work):
+        def some(number, _):
+            for i in range(group):
+                work(number * group + i)
+            return 0
+
+        lax.fori_loop(0, row_dev // group, some, 0)
+
+    def average(r):
+        scale = 1.0 / (channel(r, 0) + 1.0)
         for k in range(3):
-            mean = jnp.where(inside, channel(z, k + 1) * scale, 0.0)
-            field[k, z] = field[k, before] + mean
-        return 0
-
-    lax.fori_loop(0, drift_dev, average, 0)
-
-    def across(k, z):
-        x = field[k, z]
-        total = taps[0] * x
+            mean = jnp.where(inside, channel(r, k + 1) * scale, 0.0)
+            field[k, r + 2] = mean
+            sums[k, pl.ds(r, 1)] = jnp.sum(mean, axis=0, keepdims=True)
+
+    each_row(average)
+
+    def across(x, weight):
+        total = weight[0] * x
         for d in range(1, TAPS):
-            total += taps[d] * (pltpu.roll(x, d, 1) + pltpu.roll(x, LANES - d, 1))
-        field[k, z] = total
-
-    def down(k, z):
-        x = field[k, z]
+            total += weight[d] * (pltpu.roll(x, d, 1) + pltpu.roll(x, LANES - d, 1))
+        return total
+
+    def down(x):
         near = pltpu.roll(x, 1, 0) + pltpu.roll(x, rows_pad - 1, 0)
         far = pltpu.roll(x, 2, 0) + pltpu.roll(x, rows_pad - 2, 0)
         return 3.0 * x + 2.0 * near + far
@@ -211,14 +229,14 @@
 
     last_out[...] = jnp.zeros_like(last_out)
     for k in range(3):
-        across(k, last)
+        sums[k] = across(sums[k], taps)
         for j in range(2):
-            last_out[0, pl.ds(k * 2 + j, 1)] = field[k, last, pl.ds(j, 1)]
-            last_out[1, pl.ds(k * 2 + j, 1)] = field[k, last, pl.ds(row_dev - 2 + j, 1)]
+            last_out[0, pl.ds(k * 2 + j, 1)] = sums[k, pl.ds(j, 1)]
+            last_out[1, pl.ds(k * 2 + j, 1)] = sums[k, pl.ds(row_dev - 2 + j, 1)]
     last_low = to_low(last_out.at[0], last_in.at[1], 0)
     last_high = to_high(last_out.at[1], last_in.at[0], 1)
-    both_low = to_low(low_out, high_in, 2)
-    both_high = to_high(high_out, low_in, 3)
+    both_low = to_low(field.at[:, pl.ds(2, 2)], field.at[:, pl.ds(row_dev + 2, 2)], 2)
+    both_high = to_high(field.at[:, pl.ds(row_dev, 2)], field.at[:, pl.ds(0, 2)], 3)
 
     @pl.when(has_low)
     def _():
@@ -227,30 +245,22 @@
     @pl.when(has_high)
     def _():
         last_high.start()
-
-    def widen(z, _):
-        for k in range(3):
-            across(k, z)
-            for j in range(2):
-                low_out[j, k, pl.ds(z, 1)] = field[k, z, pl.ds(j, 1)]
-                high_out[j, k, pl.ds(z, 1)] = field[k, z, pl.ds(row_dev - 2 + j, 1)]
-        return 0
 
     @pl.when(has_high)
     def _():
         last_low.wait_recv()
         for k in range(3):
-            field[k, last, pl.ds(row_dev, 2)] = last_in[1, pl.ds(k * 2, 2)]
+            sums[k, pl.ds(row_dev, 2)] = last_in[1, pl.ds(k * 2, 2)]
 
     @pl.when(has_low)
     def _():
         last_high.wait_recv()
         for k in range(3):
-            field[k, last, pl.ds(rows_pad - 2, 2)] = last_in[0, pl.ds(k * 2, 2)]
+            sums[k, pl.ds(rows_pad - 2, 2)] = last_in[0, pl.ds(k * 2, 2)]
 
     totals[...] = jnp.zeros_like(totals)
     for k in range(3):
-        totals[pl.ds(k * rows_pad, rows_pad)] = down(k, last)
+        totals[pl.ds(k * rows_pad, rows_pad)] = down(sums[k])
 
     def first_copy(s):
         target = lax.rem(my_gz + s, gz_count)
@@ -282,7 +292,21 @@
         first_copy(s).start()
     by_gz[my_gz] = totals[pl.ds(pl.multiple_of(my_gz * part, part), part)]
 
-    lax.fori_loop(0, last, widen, 0)
+    drift_iota = lax.broadcasted_iota(jnp.int32, (drift_pad, LANES), 0)
+
+    def widen(r):
+        weight = [
+            jnp.broadcast_to(taps[d, pl.ds(r, 1)], (drift_pad, LANES)) for d in range(TAPS)
+        ]
+        for k in range(3):
+            x = across(field[k, r + 2], weight)
+            d = 1
+            while d < drift_dev:
+                x += jnp.where(drift_iota >= d, pltpu.roll(x, d, 0), 0.0)
+                d *= 2
+            field[k, r + 2] = x
+
+    each_row(widen)
 
     @pl.when(has_low)
     def _():
@@ -300,31 +324,6 @@
     by_tf[my_tf] = column
     for s in range(1, tf_count):
         second_copy(s).start()
-
-    @pl.when(has_high)
-    def _():
-        both_low.wait_recv()
-
-    @pl.when(has_low)
-    def _():
-        both_high.wait_recv()
-
-    def fill(z, _):
-        @pl.when(has_high)
-        def _():
-            for k in range(3):
-                for j in range(2):
-                    field[k, z, pl.ds(row_dev + j, 1)] = high_in[j, k, pl.ds(z, 1)]
-
-        @pl.when(has_low)
-        def _():
-            for k in range(3):
-                for j in range(2):
-                    field[k, z, pl.ds(rows_pad - 2 + j, 1)] = low_in[j, k, pl.ds(z, 1)]
-
-        return 0
-
-    lax.fori_loop(0, last, fill, 0)
 
     for s in range(1, tf_count):
         second_copy(s).wait_recv()
@@ -338,25 +337,26 @@
         third_copy(s).start()
     carry[pl.ds(pl.multiple_of(my_gz * part, part), part)] = back[my_gz]
 
-    def narrow(z, _):
+    @pl.when(has_high)
+    def _():
+        both_low.wait_recv()
+
+    @pl.when(has_low)
+    def _():
+        both_high.wait_recv()
+
+    for s in range(1, gz_count):
+        third_copy(s).wait_recv()
+
+    def finish(r):
         for k in range(3):
-            field[k, z] = down(k, z)
-        return 0
-
-    lax.fori_loop(0, last, narrow, 0)
-    for k in range(3):
-        field[k, last] = totals[pl.ds(k * rows_pad, rows_pad)]
-
-    for s in range(1, gz_count):
-        third_copy(s).wait_recv()
-
-    def finish(z, _):
-        for k in range(3):
-            whole = field[k, z] + carry[pl.ds(k * rows_pad, rows_pad)]
-            out_ref[k, z] = whole[:row_dev, :PAD]
-        return 0
-
-    lax.fori_loop(0, drift_dev, finish, 0)
+            near = field[k, r + 1] + field[k, r + 3]
+            far = field[k, r] + field[k, r + 4]
+            before = carry[pl.ds(k * rows_pad + r, 1)]
+            whole = 3.0 * field[k, r + 2] + 2.0 * near + far + before
+            out_ref[k, r] = whole[:drift_dev, :PAD]
+
+    each_row(finish)
 
     for s in range(1, tf_count):
         residual_copy(s).wait_send()
@@ -381,31 +381,34 @@
     gz_count = lax.axis_size("gz")
     sec_count = lax.axis_size("sec")
     drift_dev = DRIFT // (tf_count * gz_count)
+    drift_pad = round_up(drift_dev, 16)
     row_dev = kernel_reach.shape[0]
     rows_pad = round_up(row_dev + 4, 16)
     part = round_up(-(-3 * rows_pad // gz_count), 8)
     slots = weights.shape[-1]
     half = slots // 2
     step = min(512, half)
-    sizes = (tf_count, gz_count, sec_count, drift_dev, row_dev, rows_pad, part, half, step)
+    sizes = (
+        tf_count, gz_count, sec_count, drift_dev, drift_pad, row_dev, rows_pad, part, half, step
+    )
     reach = jnp.pad(kernel_reach, (0, rows_pad - row_dev), constant_values=1)[:, None]
     vmem = pl.BlockSpec(memory_space=pltpu.VMEM)
-    bins = round_up(drift_dev, 8)
-    return pl.pallas_call(
+    maps = pl.pallas_call(
         functools.partial(kernel, sizes),
-        out_shape=jax.ShapeDtypeStruct((3, drift_dev, row_dev, PAD), F32),
+        out_shape=jax.ShapeDtypeStruct((3, row_dev, drift_dev, PAD), F32),
         in_specs=[vmem] * 5,
         out_specs=vmem,
         scratch_shapes=[
             pltpu.VMEM((tf_count, 16, half), BF16),
             pltpu.VMEM((tf_count, 16, half), BF16),
-            pltpu.VMEM((drift_dev * rows_pad, 4 * PADS), F32),
-            pltpu.VMEM((3, drift_dev, rows_pad, LANES), F32),
+            pltpu.VMEM((row_dev * drift_pad, 2 * step), BF16),
+            pltpu.VMEM((row_dev * drift_pad, 2 * step), BF16),
+            pltpu.VMEM((4 * PADS, 2 * step), BF16),
+            pltpu.VMEM((4 * PADS, 2 * step), BF16),
+            pltpu.VMEM((row_dev * drift_pad, 4 * PADS), F32),
+            pltpu.VMEM((3, row_dev + 4, drift_pad, LANES), F32),
+            pltpu.VMEM((3, rows_pad, LANES), F32),
             pltpu.VMEM((TAPS, rows_pad, LANES), F32),
-            pltpu.VMEM((2, 3, bins, LANES), F32),
-            pltpu.VMEM((2, 3, bins, LANES), F32),
-            pltpu.VMEM((2, 3, bins, LANES), F32),
-            pltpu.VMEM((2, 3, bins, LANES), F32),
             pltpu.VMEM((2, 8, LANES), F32),
             pltpu.VMEM((2, 8, LANES), F32),
             pltpu.VMEM((gz_count * part, LANES), F32),
@@ -430,6 +433,7 @@
         voxels[:, 0, 0, 0],
         reach,
     )
+    return jnp.transpose(maps, (0, 2, 1, 3))
 
 
 def solution(mesh):

time: 113 us -> 107 us (0.947)
  Pallas kernels: 105 us -> 101 us
  local copies, waits for them, and re-layouts: 7.51 us -> 5.67 us
    pallas_call x1 -> x0, local copies, waits for them, and re-layouts: 6.14 us -> none  [per_device(): pl.pallas_call(functools.partial(kernel, sizes), out_shape=jax.ShapeDtype...]
    unnamed x0 -> x1, local copies, waits for them, and re-layouts: none -> 4.3 us
    pallas_call x1, Pallas kernels: 105 us -> 101 us  [per_device(): pl.pallas_call(functools.partial(kernel, sizes), out_shape=jax.ShapeDtype...]
where the time goes in v2:
time: 107 us
  Pallas kernels  101 us (94%)
  local copies, waits for them, and re-layouts  5.67 us (5%)
    pallas_call x1, Pallas kernels, per_device(): pl.pallas_call(functools.partial(kernel, sizes), out_shape=jax.ShapeDtype...  101 us
    unnamed x1, local copies, waits for them, and re-layouts  4.3 us

profile of v2, /device:TPU:0, one launch (start us, length us, event | category | flops | bytes accessed | tf_op | source)
XLA Modules:
  0.0 106.7 jit_solution(10645282735605233371)
XLA Ops:
  0.0 0.7 pad_bitcast_fusion
  0.7 0.7 copy.6.reach_ref
  1.4 101.0 %shard_map.55 = f32[3,76,16,180]{3,2,1,0:T(8,128)} custom-call(bf16[3,4,8192]{2,1,0:T(4,128)(2,1)} %bitcast.9, bf16[4,8192]{1,0:T(4,128)(2,1)} %bitcast.10, bf16[4,8192]{1,0:T(4,128)(2,1)} %bitcast.11, s32[3,4,8192]{2,1,0:T(4,128)} %bitcast.8, s32[80,1]{1,0:T(8,128)} %copy.6.reach_ref), custom_call_target="tpu_custom_call" | custom-call | tf_op jit(solution)/shard_map/pallas_call | solution.py:396
  102.4 4.3 %copy.8 = f32[3,16,76,180]{3,1,2,0:T(8,128)} copy(f32[3,16,76,180]{3,1,2,0:T(8,128)} %bitcast.7) | data formatting | bytes 5253120

commit v3 on v2

--- a/solution.py
+++ b/solution.py
@@ -29,6 +29,7 @@
     vox_ref,
     reach_ref,
     out_ref,
+    carry,
     send_buf,
     recv_buf,
     cells_even,
@@ -45,13 +46,14 @@
     by_gz,
     by_tf,
     back,
-    carry,
+    local,
     res_send,
     res_recv,
     halo_send,
     halo_recv,
     scan_send,
     scan_recv,
+    out_sem,
 ):
     tf_count, gz_count, sec_count, drift_dev, drift_pad, row_dev, rows_pad, part, half, step = sizes
     my_tf = lax.axis_index("tf")
@@ -59,7 +61,6 @@
     my_sec = lax.axis_index("sec")
     has_low = my_sec > 0
     has_high = my_sec < sec_count - 1
-    group = 4 if row_dev % 4 == 0 else 1
 
     for r in (0, 1, row_dev + 2, row_dev + 3):
         field[:, r] = jnp.zeros((3, drift_pad, LANES), F32)
@@ -112,7 +113,12 @@
     recv_buf[0] = send_buf[my_tf]
     hist[...] = jnp.zeros_like(hist)
 
-    reach = reach_ref[...].astype(F32)
+    square = (rows_pad, row_dev)
+    diagonal = lax.broadcasted_iota(jnp.int32, square, 0) == lax.broadcasted_iota(
+        jnp.int32, square, 1
+    )
+    reach = jnp.broadcast_to(reach_ref[...].astype(F32), square)
+    reach = jnp.sum(jnp.where(diagonal, reach, 0.0), axis=1, keepdims=True)
     spread = jnp.broadcast_to(reach, (rows_pad, LANES)) + 1.0
     for d in range(TAPS):
         taps[d] = jnp.maximum(spread - float(d), 0.0) / (spread * spread * 9.0)
@@ -187,13 +193,15 @@
             piece = pltpu.roll(piece, LANES - (c * PADS - start), 1)
         return piece
 
-    def each_row(work):
+    def each_row(work, first, count):
+        group = 4 if count % 4 == 0 else 1
+
         def some(number, _):
             for i in range(group):
-                work(number * group + i)
+                work(first + number * group + i)
             return 0
 
-        lax.fori_loop(0, row_dev // group, some, 0)
+        lax.fori_loop(0, count // group, some, 0)
 
     def average(r):
         scale = 1.0 / (channel(r, 0) + 1.0)
@@ -202,7 +210,7 @@
             field[k, r + 2] = mean
             sums[k, pl.ds(r, 1)] = jnp.sum(mean, axis=0, keepdims=True)
 
-    each_row(average)
+    each_row(average, 0, row_dev)
 
     def across(x, weight):
         total = weight[0] * x
@@ -306,7 +314,8 @@
                 d *= 2
             field[k, r + 2] = x
 
-    each_row(widen)
+    for r in (0, 1, row_dev - 2, row_dev - 1):
+        widen(r)
 
     @pl.when(has_low)
     def _():
@@ -315,6 +324,9 @@
     @pl.when(has_high)
     def _():
         both_high.start()
+
+    early = (row_dev - 4) * 5 // 36 * 4
+    each_row(widen, 2, early)
 
     for s in range(1, gz_count):
         first_copy(s).wait_recv()
@@ -324,6 +336,7 @@
     by_tf[my_tf] = column
     for s in range(1, tf_count):
         second_copy(s).start()
+    each_row(widen, 2 + early, row_dev - 4 - early)
 
     for s in range(1, tf_count):
         second_copy(s).wait_recv()
@@ -345,18 +358,19 @@
     def _():
         both_high.wait_recv()
 
-    for s in range(1, gz_count):
-        third_copy(s).wait_recv()
-
     def finish(r):
         for k in range(3):
             near = field[k, r + 1] + field[k, r + 3]
             far = field[k, r] + field[k, r + 4]
-            before = carry[pl.ds(k * rows_pad + r, 1)]
-            whole = 3.0 * field[k, r + 2] + 2.0 * near + far + before
-            out_ref[k, r] = whole[:drift_dev, :PAD]
-
-    each_row(finish)
+            whole = 3.0 * field[k, r + 2] + 2.0 * near + far
+            local[k, r] = whole[:drift_dev, :PAD]
+
+    each_row(finish, 0, row_dev)
+    result = pltpu.make_async_copy(local, out_ref, out_sem)
+    result.start()
+    for s in range(1, gz_count):
+        third_copy(s).wait_recv()
+    result.wait()
 
     for s in range(1, tf_count):
         residual_copy(s).wait_send()
@@ -387,17 +401,19 @@
     part = round_up(-(-3 * rows_pad // gz_count), 8)
     slots = weights.shape[-1]
     half = slots // 2
-    step = min(512, half)
+    step = min(1024, half)
     sizes = (
         tf_count, gz_count, sec_count, drift_dev, drift_pad, row_dev, rows_pad, part, half, step
     )
-    reach = jnp.pad(kernel_reach, (0, rows_pad - row_dev), constant_values=1)[:, None]
     vmem = pl.BlockSpec(memory_space=pltpu.VMEM)
-    maps = pl.pallas_call(
+    maps, carry = pl.pallas_call(
         functools.partial(kernel, sizes),
-        out_shape=jax.ShapeDtypeStruct((3, row_dev, drift_dev, PAD), F32),
+        out_shape=(
+            jax.ShapeDtypeStruct((3, row_dev, drift_dev, PAD), F32),
+            jax.ShapeDtypeStruct((gz_count * part, LANES), F32),
+        ),
         in_specs=[vmem] * 5,
-        out_specs=vmem,
+        out_specs=(pl.BlockSpec(memory_space=pl.ANY), vmem),
         scratch_shapes=[
             pltpu.VMEM((tf_count, 16, half), BF16),
             pltpu.VMEM((tf_count, 16, half), BF16),
@@ -415,13 +431,14 @@
             pltpu.VMEM((gz_count, part, LANES), F32),
             pltpu.VMEM((tf_count, part, LANES), F32),
             pltpu.VMEM((gz_count, part, LANES), F32),
-            pltpu.VMEM((gz_count * part, LANES), F32),
+            pltpu.VMEM((3, row_dev, drift_dev, PAD), F32),
             pltpu.SemaphoreType.DMA((tf_count,)),
             pltpu.SemaphoreType.DMA((tf_count,)),
             pltpu.SemaphoreType.DMA((4,)),
             pltpu.SemaphoreType.DMA((4,)),
             pltpu.SemaphoreType.DMA((3, max(tf_count, gz_count))),
             pltpu.SemaphoreType.DMA((3, max(tf_count, gz_count))),
+            pltpu.SemaphoreType.DMA,
         ],
         compiler_params=pltpu.CompilerParams(
             collective_id=0, has_side_effects=True, vmem_limit_bytes=56 * 1024 * 1024
@@ -431,9 +448,10 @@
         weights[0, 0, 0],
         fraction[0, 0, 0],
         voxels[:, 0, 0, 0],
-        reach,
+        kernel_reach[None, :],
     )
-    return jnp.transpose(maps, (0, 2, 1, 3))
+    carry = carry[: 3 * rows_pad].reshape(3, rows_pad, LANES)[:, :row_dev, :PAD]
+    return jnp.transpose(maps + carry[:, :, None], (0, 2, 1, 3))
 
 
 def solution(mesh):

time: 107 us -> 101 us (0.944)
  Pallas kernels: 101 us -> 95 us
  local copies, waits for them, and re-layouts: 5.67 us -> 0.96 us
  other arithmetic: 0 us -> 4.61 us
    pallas_call x1, Pallas kernels: 101 us -> 95 us  [per_device(): pl.pallas_call(functools.partial(kernel, sizes), out_shape=(jax.ShapeDtyp...]
    transpose x0 -> x1, other arithmetic: none -> 4.61 us  [per_device(): return jnp.transpose(maps + carry[:, :, None], (0, 2, 1, 3))]
    unnamed x1 -> x0, local copies, waits for them, and re-layouts: 4.3 us -> none
    broadcast_in_dim x2 -> x0, local copies, waits for them, and re-layouts: 1.38 us -> none  [per_device(): jnp.pad(kernel_reach, (0, rows_pad - row_dev), constant_values=1)[:, None]]
where the time goes in v3:
time: 101 us
  Pallas kernels  95 us (94%)
  other arithmetic  4.61 us (5%)
    pallas_call x1, Pallas kernels, per_device(): pl.pallas_call(functools.partial(kernel, sizes), out_shape=(jax.ShapeDtyp...  95 us
    transpose x1, other arithmetic, per_device(): return jnp.transpose(maps + carry[:, :, None], (0, 2, 1, 3))  4.61 us

profile of v3, /device:TPU:0, one launch (start us, length us, event | category | flops | bytes accessed | tf_op | source)
XLA Modules:
  0.0 100.6 jit_solution(4593447464828797334)
XLA Ops:
  0.0 95.0 %shard_map.55 = (f32[3,76,16,180]{3,2,1,0:T(8,128)}, f32[256,256]{1,0:T(8,128)}) custom-call(bf16[3,4,8192]{2,1,0:T(4,128)(2,1)} %bitcast.11, bf16[4,8192]{1,0:T(4,128)(2,1)} %bitcast.12, bf16[4,8192]{1,0:T(4,128)(2,1)} %bitcast.13, s32[3,4,8192]{2,1,0:T(4,128)} %bitcast.10, s32[1,76]{1,0:T(1,128)} %bitcast.14), custom_call_target="tpu_custom_call" | custom-call | tf_op jit(solution)/shard_map/pallas_call | solution.py:409
  95.0 1.0 slice.6
  96.0 4.6 %add_bitcast_fusion = f32[3,16,76,180]{3,1,2,0:T(8,128)} fusion(f32[3,76,16,180]{3,2,1,0:T(8,128)} %get-tuple-element.7, f32[3,76,180]{2,1,0:T(8,128)S(1)} %bitcast.9), kind=kLoop, calls=%fused_computation | loop fusion | flops 656640 | bytes 5417280 | tf_op jit(solution)/shard_map/transpose | solution.py:454

commit v4 on v3

--- a/solution.py
+++ b/solution.py
@@ -29,7 +29,7 @@
     vox_ref,
     reach_ref,
     out_ref,
-    carry,
+    carry_ref,
     send_buf,
     recv_buf,
     cells_even,
@@ -46,6 +46,7 @@
     by_gz,
     by_tf,
     back,
+    carry,
     local,
     res_send,
     res_recv,
@@ -266,9 +267,16 @@
         for k in range(3):
             sums[k, pl.ds(rows_pad - 2, 2)] = last_in[0, pl.ds(k * 2, 2)]
 
+    all_rows = 3 * rows_pad
+    mid = all_rows // 2
+    whole_sums = jnp.concatenate([down(sums[k]) for k in range(3)], axis=0)
     totals[...] = jnp.zeros_like(totals)
-    for k in range(3):
-        totals[pl.ds(k * rows_pad, rows_pad)] = down(sums[k])
+    totals[:all_rows] = whole_sums[:, :128]
+    upper = whole_sums[:, 128:]
+    pair_lane = lax.broadcasted_iota(jnp.int32, (mid, 128), 1)
+    totals[all_rows : all_rows + mid] = jnp.where(
+        pair_lane < 64, upper[:mid], pltpu.roll(upper[mid:], 64, 1)
+    )
 
     def first_copy(s):
         target = lax.rem(my_gz + s, gz_count)
@@ -340,7 +348,7 @@
 
     for s in range(1, tf_count):
         second_copy(s).wait_recv()
-    base = jnp.zeros((part, LANES), F32)
+    base = jnp.zeros((part, 128), F32)
     for t in range(tf_count):
         base += jnp.where(t < my_tf, by_tf[t], 0.0)
     for g in range(gz_count):
@@ -370,6 +378,12 @@
     result.start()
     for s in range(1, gz_count):
         third_copy(s).wait_recv()
+    pairs = carry[all_rows : all_rows + mid]
+    upper = jnp.concatenate([pairs, pltpu.roll(pairs, 64, 1)], axis=0)
+    for k in range(3):
+        rows = slice(k * rows_pad, k * rows_pad + row_dev)
+        carry_ref[k, :, :128] = carry[rows]
+        carry_ref[k, :, 128:] = upper[rows, : PAD - 128]
     result.wait()
 
     for s in range(1, tf_count):
@@ -398,7 +412,7 @@
     drift_pad = round_up(drift_dev, 16)
     row_dev = kernel_reach.shape[0]
     rows_pad = round_up(row_dev + 4, 16)
-    part = round_up(-(-3 * rows_pad // gz_count), 8)
+    part = round_up(-(-9 * rows_pad // (2 * gz_count)), 8)
     slots = weights.shape[-1]
     half = slots // 2
     step = min(1024, half)
@@ -410,7 +424,7 @@
         functools.partial(kernel, sizes),
         out_shape=(
             jax.ShapeDtypeStruct((3, row_dev, drift_dev, PAD), F32),
-            jax.ShapeDtypeStruct((gz_count * part, LANES), F32),
+            jax.ShapeDtypeStruct((3, row_dev, PAD), F32),
         ),
         in_specs=[vmem] * 5,
         out_specs=(pl.BlockSpec(memory_space=pl.ANY), vmem),
@@ -427,10 +441,11 @@
             pltpu.VMEM((TAPS, rows_pad, LANES), F32),
             pltpu.VMEM((2, 8, LANES), F32),
             pltpu.VMEM((2, 8, LANES), F32),
-            pltpu.VMEM((gz_count * part, LANES), F32),
-            pltpu.VMEM((gz_count, part, LANES), F32),
-            pltpu.VMEM((tf_count, part, LANES), F32),
-            pltpu.VMEM((gz_count, part, LANES), F32),
+            pltpu.VMEM((gz_count * part, 128), F32),
+            pltpu.VMEM((gz_count, part, 128), F32),
+            pltpu.VMEM((tf_count, part, 128), F32),
+            pltpu.VMEM((gz_count, part, 128), F32),
+            pltpu.VMEM((gz_count * part, 128), F32),
             pltpu.VMEM((3, row_dev, drift_dev, PAD), F32),
             pltpu.SemaphoreType.DMA((tf_count,)),
             pltpu.SemaphoreType.DMA((tf_count,)),
@@ -441,7 +456,7 @@
             pltpu.SemaphoreType.DMA,
         ],
         compiler_params=pltpu.CompilerParams(
-            collective_id=0, has_side_effects=True, vmem_limit_bytes=56 * 1024 * 1024
+            collective_id=0, has_side_effects=True, vmem_limit_bytes=40 * 1024 * 1024
         ),
     )(
         residuals[:, 0, 0, 0],
@@ -450,7 +465,6 @@
         voxels[:, 0, 0, 0],
         kernel_reach[None, :],
     )
-    carry = carry[: 3 * rows_pad].reshape(3, rows_pad, LANES)[:, :row_dev, :PAD]
     return jnp.transpose(maps + carry[:, :, None], (0, 2, 1, 3))
 
 

time: 101 us -> 97.7 us (0.967)
  Pallas kernels: 95 us -> 90.7 us
  local copies, waits for them, and re-layouts: 0.96 us -> 4.25 us
  other arithmetic: 4.61 us -> 2.43 us
    pallas_call x1, Pallas kernels: 95 us -> 90.7 us  [per_device(): pl.pallas_call(functools.partial(kernel, sizes), out_shape=(jax.ShapeDtyp...]
    unnamed x0 -> x10, local copies, waits for them, and re-layouts: none -> 4.25 us
    transpose x1, other arithmetic: 4.61 us -> 2.43 us  [per_device(): return jnp.transpose(maps + carry[:, :, None], (0, 2, 1, 3))]
where the time goes in v4:
time: 97.7 us; the launch traced here: 97.4 us
  Pallas kernels  90.7 us (93%)
  local copies, waits for them, and re-layouts  4.25 us (4%)
  other arithmetic  2.43 us (2%)
    pallas_call x1, Pallas kernels, per_device(): pl.pallas_call(functools.partial(kernel, sizes), out_shape=(jax.ShapeDtyp...  90.7 us
    unnamed x10, local copies, waits for them, and re-layouts  4.25 us
    transpose x1, other arithmetic, per_device(): return jnp.transpose(maps + carry[:, :, None], (0, 2, 1, 3))  2.43 us

profile of v4, /device:TPU:0, one launch (start us, length us, event | category | flops | bytes accessed | tf_op | source)
XLA Modules:
  0.0 97.4 jit_solution(13046771722378630269)
XLA Ops:
  0.0 0.0 copy-start
  0.0 1.0 %copy-done = s32[3,1,1,1,4,8192]{5,4,3,2,1,0:T(4,128)S(1)} copy-done((s32[3,1,1,1,4,8192]{5,4,3,2,1,0:T(4,128)S(1)}, s32[3,1,1,1,4,8192]{5,4,3,2,1,0:T(4,128)}, u32[]{:S(2)}) %copy-start) | copy-done | bytes 393240
  1.0 0.0 copy-start.1
  1.0 0.9 copy-done.1
  1.9 0.0 copy-start.2
  1.9 0.8 copy-done.2
  2.8 0.0 copy-start.3
  2.8 0.8 copy-done.3
  3.6 0.0 copy-start.4
  3.6 0.7 copy-done.4
  4.3 90.7 %shard_map.55 = (f32[3,76,16,180]{3,2,1,0:T(8,128)S(1)}, f32[3,76,180]{2,1,0:T(8,128)S(1)}) custom-call(bf16[3,4,8192]{2,1,0:T(4,128)(2,1)S(1)} %bitcast.8, bf16[4,8192]{1,0:T(4,128)(2,1)S(1)} %bitcast.9, bf16[4,8192]{1,0:T(4,128)(2,1)S(1)} %bitcast.10, s32[3,4,8192]{2,1,0:T(4,128)S(1)} %bitcast.7, s32[1,76]{1,0:T(1,128)S(1)} %bitcast.11), custom_call_target="tpu_custom_call" | custom-call | tf_op jit(solution)/shard_map/pallas_call | solution.py:423
  94.9 2.4 %add_bitcast_fusion = f32[3,16,76,180]{3,1,2,0:T(8,128)} fusion(f32[3,76,16,180]{3,2,1,0:T(8,128)S(1)} %get-tuple-element.7, f32[3,76,180]{2,1,0:T(8,128)S(1)} %get-tuple-element.8), kind=kLoop, calls=%fused_computation | loop fusion | flops 656640 | bytes 5417280 | tf_op jit(solution)/shard_map/transpose | solution.py:468
Async XLA Ops:
  0.0 1.0 %copy-start = (s32[3,1,1,1,4,8192]{5,4,3,2,1,0:T(4,128)S(1)}, s32[3,1,1,1,4,8192]{5,4,3,2,1,0:T(4,128)}, u32[]{:S(2)}) copy-start(s32[3,1,1,1,4,8192]{5,4,3,2,1,0:T(4,128)} %param.8) | copy-start | bytes 1179652
  1.0 0.9 copy-start.1
  1.9 0.8 copy-start.2
  2.8 0.8 copy-start.3
  3.6 0.7 copy-start.4
